TPU v7x, 32 devices: a whole 2x2x4 slice. The times are simulated.
32 devices in a mesh: phase: 2 (over x), seq: 16 (over z, y, core).
Axes of the slice: x: 2, y: 2, z: 4, core: 2. Of those that a mesh axis runs over, the one named last changes fastest.
Arguments:
- tokens: bfloat16 [1024, 1024], P('seq'), may hold values from -6 to 6
- phase_weight: bfloat16 [2, 1024, 1024], P('phase'), may hold values from -0.1875 to 0.1875
- phase_gain: float32 [2, 1024], P('phase'), may hold values from 0.25 to 1.75
- unit_weight: bfloat16 [1024, 1024], replicated, may hold values from -0.1875 to 0.1875
- unit_gain: float32 [1024], replicated, may hold values from 0.25 to 1.75
- durations: int32 [1024], P('seq'), may hold values from 4 to 32, as said below
Outputs:
- encoder_out: bfloat16 [1024, 1024], P('seq')
- unit_states: bfloat16 [8192, 1024], P(('phase', 'seq'))
Inputs may be any that keep to these rules, and one draw needn't show every extreme that they name: durations sum to 8192; some token has exactly 32 frames and some exactly 4.
All inputs are finite; a program needn't handle non-finite values.
Results may differ from a plain program's by a relative error of at most 0.0062.
Values may be sent and summed in bfloat16 or wider, within the bound.
A program may use at most 64 MiB of HBM per device.

v0:
```python
import jax
import jax.numpy as jnp
from jax import lax
from jax.sharding import PartitionSpec as P

FR_DEV = 256


def from_behind(block, axis, distance):
    devices = range(lax.axis_size(axis))
    route = [(i - distance, i) for i in devices if i - distance in devices]
    return lax.ppermute(block, axis, route)


def from_root(array, axis, root):
    mine = lax.axis_index(axis) == root
    return lax.psum(jnp.where(mine, array, jnp.zeros_like(array)), axis)


def carried_in(array, axis, combine, identity):
    peers, mine = (lax.axis_size(axis), lax.axis_index(axis))
    everything = lax.all_gather(array, axis)
    start = jnp.broadcast_to(jnp.asarray(identity, array.dtype), array.shape)

    def turn(k, before):
        reached = k < mine
        new = combine(before, everything[k])
        return jnp.where(reached, new, before)

    return lax.fori_loop(0, peers, turn, start)


def layer(values_in, weight, gain):
    widened = values_in.astype(jnp.float32)
    scaled = widened * gain / jnp.sqrt(jnp.mean(widened * widened, axis=-1, keepdims=True) + 1e-06)
    normed = scaled.astype(jnp.bfloat16)
    branch = jax.nn.silu(jnp.dot(normed, weight, preferred_element_type=jnp.float32))
    return (widened + branch).astype(jnp.bfloat16)


def shards(tokens, phase_weight, phase_gain, unit_weight, unit_gain, durations):
    weight = phase_weight[0]
    gain_row = phase_gain[0]
    phases = lax.axis_size("phase")
    seqsize = lax.axis_size("seq")
    phase_index = lax.axis_index("phase")

    def whole_step(turn_index, current):
        return from_behind(layer(current, weight, gain_row), "phase", 1)

    hidden = layer(lax.fori_loop(0, phases - 1, whole_step, tokens), weight, gain_row)
    hidden = from_root(hidden, "phase", phases - 1)
    offset = carried_in(
        jnp.sum(durations), "seq", lambda earlier, latest: earlier + latest, jnp.int32(0)
    )
    frame_ends = offset + jnp.cumsum(durations)
    begins = frame_ends - durations
    first_frame = (phase_index * seqsize + lax.axis_index("seq")) * FR_DEV
    frames = first_frame + lax.iota(jnp.int32, FR_DEV)
    tok_count = durations.shape[0]
    min_frames = max(phases * FR_DEV // (2 * tok_count), 1)
    slot_count = min(tok_count, (FR_DEV - 2) // min_frames + 2)
    frame_low = (phase_index * seqsize + lax.iota(jnp.int32, seqsize)) * FR_DEV
    frame_high = frame_low + FR_DEV
    firsts = jnp.sum((frame_ends[None, :] <= frame_low[:, None]).astype(jnp.int32), axis=1)
    wanted = (firsts[:, None] + lax.iota(jnp.int32, slot_count)[None, :]).reshape(-1)
    clamped = jnp.minimum(wanted, tok_count - 1)
    usable = (wanted < tok_count) & (begins[clamped] < jnp.repeat(frame_high, slot_count))
    send_rows = jnp.where(usable[:, None], hidden[clamped], jnp.zeros((), jnp.bfloat16))
    send_begin = jnp.where(usable, begins[clamped], 0).astype(jnp.int32)
    send_end = jnp.where(usable, frame_ends[clamped], 0).astype(jnp.int32)
    got_rows, got_begin, got_end = (
        lax.all_to_all(send_rows, "seq", split_axis=0, concat_axis=0, tiled=True),
        lax.all_to_all(send_begin, "seq", split_axis=0, concat_axis=0, tiled=True),
        lax.all_to_all(send_end, "seq", split_axis=0, concat_axis=0, tiled=True),
    )
    member = (frames[:, None] >= got_begin[None, :]) & (frames[:, None] < got_end[None, :])
    expanded = jnp.dot(
        member.astype(jnp.bfloat16), got_rows, preferred_element_type=jnp.float32
    ).astype(jnp.bfloat16)
    unit_states = layer(expanded, unit_weight, unit_gain)
    return (hidden, unit_states)


def solution(mesh):
    return jax.shard_map(
        shards,
        mesh=mesh,
        in_specs=(P("seq", None), P("phase", None, None), P("phase", None), P(), P(), P("seq")),
        out_specs=(P("seq", None), P(("phase", "seq"), None)),
        check_vma=False,
    )
```

profile of v0, /device:TPU:13, one launch (start us, length us, event | category | flops | bytes accessed | tf_op | source)
XLA Modules:
  0.0 257.4 jit_solution(7181134546518761841)
XLA Ops:
  7.2 1.5 reduce_sum.48
  8.7 1.2 dynamic-slice
  9.9 1.4 dynamic-update-slice
  11.3 7.9 %all-reduce = s32[16]{0:T(128)S(1)} all-reduce(s32[16]{0:T(128)S(1)} %dynamic-update-slice), channel_id=1, replica_groups=mesh['phase'=2,'seq'=16] {'seq'}, use_global_device_ids=true, to_apply=%add | all-reduce | flops 16 | bytes 128
  19.2 22.2 %while.8 = (s32[]{:T(128)}, s32[]{:T(128)}, s32[]{:T(128)}, s32[16]{0:T(128)S(1)}, s32[]{:T(128)}) while((s32[]{:T(128)}, s32[]{:T(128)}, s32[]{:T(128)}, s32[16]{0:T(128)S(1)}, s32[]{:T(128)}) %tuple.221), condition=%wide.region_5.6_spmd, body=%wide.region_4.5_spmd.sunk | while | flops 5 | bytes 115 | solution.py:30
  41.4 0.7 copy.13
  44.4 0.7 fusion.52
  45.2 0.7 fusion.54
  48.9 40.1 %select_select_fusion = (s32[1024]{0:T(1024)S(1)}, pred[1024]{0:T(1024)(128)(4,1)S(1)}, pred[1024]{0:T(1024)(128)(4,1)S(1)}, pred[1024]{0:T(1024)(128)(4,1)S(1)}...) fusion(s32[]{:T(128)} %bitcast.72, s32[]{:T(128)} %bitcast.73, ...), kind=kLoop, calls=%fused_computation.53 | loop fusion | flops 129024 | bytes 72960 | tf_op jit(solution)/shard_map/gather | solution.py:71
  89.0 40.0 %select_select_fusion.1 = s32[1024]{0:T(1024)S(1)} fusion(pred[1024]{0:T(1024)(128)(4,1)S(1)} %get-tuple-element.165, pred[1024]{0:T(1024)(128)(4,1)S(1)} %get-tuple-element.164, pred[1024]{0:T(1024)(128)(4,1)S(1)} %get-tuple-element.163, pred[1024]{0:T(1024)(128)(4,1)S(1)} %get-tuple-element.162, pred[1024]{0:T(1024)(128)(4,1)S(1)} %get-tuple-element.161, ...), kind=kLoop, calls=%fused_computation.54 | loop fusion | flops 64512 | bytes 68864 | tf_op jit(solution)/shard_map/gather | solution.py:68
  129.7 8.4 %all-to-all-start.1 = ((s32[16,64,1]{1,2,0:T(1,128)}), s32[16,64,1]{1,2,0:T(1,128)S(1)}, u32[]{:S(2)}, u32[]{:S(2)}) async-start(s32[16,64,1]{1,2,0:T(1,128)} %bitcast.136), calls=%async_computation.1 | async-start | bytes 16384 | tf_op jit(solution)/shard_map/all_to_all | solution.py:75
  138.2 1.0 fusion.22
  139.3 2.3 fusion.23
  141.5 3.1 %collective-permute-start = (bf16[64,1024]{1,0:T(8,128)(2,1)S(1)}, bf16[64,1024]{1,0:T(8,128)(2,1)S(1)}, u32[]{:S(2)}, u32[]{:S(2)}) collective-permute-start(bf16[64,1024]{1,0:T(8,128)(2,1)S(1)} %fusion.23), channel_id=1, source_target_pairs={{0,16},{1,17},{2,18},{3,19},{4,20},{5,21},{6,22},{7,23},{8,24},{9,... | collective-permute-start | bytes 393224 | tf_op jit(solution)/shard_map/while/body/eval_jaxpr/ppermute | solution.py:12
  144.8 2.3 collective-permute-done
  147.3 2.8 %fusion.30 = bf16[64,1024]{1,0:T(8,128)(2,1)} fusion(bf16[1,1024,1024]{2,1,0:T(8,128)(2,1)} %param.9, bf16[64,1024]{1,0:T(8,128)(2,1)S(1)} %collective-permute-done, f32[64]{0:T(128)S(1)} %add_sqrt_fusion.1, f32[1024]{0:T(1024)S(1)} %bitcast.160, pred[]{:T(512)S(6)} %eq.3), kind=kOutput, calls=%fused_computation.37 | convolution fusion | flops 135004160 | bytes 2363649 | tf_op jit(solution)/shard_map/dot_general | solution.py:37
  150.2 23.6 %all-reduce.3.cloned.1.call-done = bf16[64,1024]{1,0:T(8,128)(2,1)} async-done(((bf16[64,1024]{1,0:T(8,128)(2,1)}), bf16[64,1024]{1,0:T(8,128)(2,1)}) %all-reduce.3.cloned.1.call-update) | async-done | bytes 131088 | tf_op jit(solution)/shard_map/psum | solution.py:17
  173.7 7.0 %gather_fusion = bf16[1024,1024]{1,0:T(8,128)(2,1)} fusion(bf16[64,1024]{1,0:T(8,128)(2,1)} %all-reduce.3.cloned.1.call-done, s32[1024]{0:T(1024)S(1)} %broadcast_clamp_fusion), kind=kCustom, calls=%fused_computation | custom fusion | bytes 4198400 | tf_op jit(solution)/shard_map/gather | solution.py:69
  180.7 6.8 %all-to-all-start = ((s32[16,64,1]{1,2,0:T(1,128)}), s32[16,64,1]{1,2,0:T(1,128)S(1)}, u32[]{:S(2)}, u32[]{:S(2)}) async-start(s32[16,64,1]{1,2,0:T(1,128)} %bitcast.71), calls=%async_computation | async-start | bytes 16384 | tf_op jit(solution)/shard_map/all_to_all | solution.py:74
  187.5 3.2 %broadcast_select_fusion = bf16[16,64,1024]{2,1,0:T(8,128)(2,1)} fusion(bf16[16,64,1024]{2,1,0:T(8,128)(2,1)} %bitcast.155, pred[16,64]{1,0:T(8,128)(4,1)S(1)} %fusion.44), kind=kLoop, calls=%fused_computation.5 | loop fusion | flops 1048576 | bytes 4195328 | tf_op jit(solution)/shard_map/jit(_where)/select_n | solution.py:69
  191.3 6.9 %all-to-all-start.2 = ((bf16[16,64,1024]{2,1,0:T(8,128)(2,1)}), bf16[16,64,1024]{2,1,0:T(8,128)(2,1)}, u32[]{:S(2)}, u32[]{:S(2)}) async-start(bf16[16,64,1024]{2,1,0:T(8,128)(2,1)} %broadcast_select_fusion), calls=%async_computation.2 | async-start | bytes 4194304 | tf_op jit(solution)/shard_map/all_to_all | solution.py:73
  200.2 45.5 %all-to-all-done.2 = bf16[16,64,1024]{2,1,0:T(8,128)(2,1)} async-done(((bf16[16,64,1024]{2,1,0:T(8,128)(2,1)}), bf16[16,64,1024]{2,1,0:T(8,128)(2,1)}, u32[]{:S(2)}, u32[]{:S(2)}) %all-to-all-start.2) | async-done | bytes 2097184 | tf_op jit(solution)/shard_map/all_to_all | solution.py:73
  245.7 2.4 fusion.6
  248.2 1.7 fusion.7
  (60 shorter events, 20.3 us)
Async XLA Ops:
  7.2 241.0 %copy-start = (bf16[1024,1024]{1,0:T(8,128)(2,1)S(1)}, bf16[1024,1024]{1,0:T(8,128)(2,1)}, u32[]{:S(2)}) copy-start(bf16[1024,1024]{1,0:T(8,128)(2,1)} %param.11) | copy-start | bytes 6291460
  89.0 58.3 %copy-start.2 = (f32[1,1024]{1,0:T(1,128)S(1)}, f32[1,1024]{1,0:T(1,128)}, u32[]{:S(2)}) copy-start(f32[1,1024]{1,0:T(1,128)} %param.10) | copy-start | bytes 12292
  129.7 51.0 %all-to-all-start.1 = ((s32[16,64,1]{1,2,0:T(1,128)}), s32[16,64,1]{1,2,0:T(1,128)S(1)}, u32[]{:S(2)}, u32[]{:S(2)}) async-start(s32[16,64,1]{1,2,0:T(1,128)} %bitcast.136), calls=%async_computation.1 | async-start | bytes 16384 | tf_op jit(solution)/shard_map/all_to_all | solution.py:75
  138.2 35.6 %all-reduce.3.cloned.1.call-start = ((), (), s32[]{:S(2)}) async-start(), calls=%async_computation.3 | async-start | bytes 262144 | tf_op jit(solution)/shard_map/psum | solution.py:17
  141.5 5.6 %collective-permute-start = (bf16[64,1024]{1,0:T(8,128)(2,1)S(1)}, bf16[64,1024]{1,0:T(8,128)(2,1)S(1)}, u32[]{:S(2)}, u32[]{:S(2)}) collective-permute-start(bf16[64,1024]{1,0:T(8,128)(2,1)S(1)} %fusion.23), channel_id=1, source_target_pairs={{0,16},{1,17},{2,18},{3,19},{4,20},{5,21},{6,22},{7,23},{8,24},{9,... | collective-permute-start | bytes 393224 | tf_op jit(solution)/shard_map/while/body/eval_jaxpr/ppermute | solution.py:12
  180.7 10.5 %all-to-all-start = ((s32[16,64,1]{1,2,0:T(1,128)}), s32[16,64,1]{1,2,0:T(1,128)S(1)}, u32[]{:S(2)}, u32[]{:S(2)}) async-start(s32[16,64,1]{1,2,0:T(1,128)} %bitcast.71), calls=%async_computation | async-start | bytes 16384 | tf_op jit(solution)/shard_map/all_to_all | solution.py:74
  191.3 54.4 %all-to-all-start.2 = ((bf16[16,64,1024]{2,1,0:T(8,128)(2,1)}), bf16[16,64,1024]{2,1,0:T(8,128)(2,1)}, u32[]{:S(2)}, u32[]{:S(2)}) async-start(bf16[16,64,1024]{2,1,0:T(8,128)(2,1)} %broadcast_select_fusion), calls=%async_computation.2 | async-start | bytes 4194304 | tf_op jit(solution)/shard_map/all_to_all | solution.py:73
  198.7 49.5 %copy-start.3 = (f32[1024]{0:T(1024)S(1)}, f32[1024]{0:T(1024)}, u32[]{:S(2)}) copy-start(f32[1024]{0:T(1024)} %param.12) | copy-start | bytes 12292
  248.2 1.7 copy-start.1
Sparse Core Ops, SparseCore 0:
  150.3 23.4 all-reduce.2
where the time goes:
time: 259 us; the launch traced here: 257 us
  other arithmetic  89.2 us (34%)
  waiting for transfers between devices  72 us (28%)
  local copies, waits for them, and re-layouts  28 us (11%)
  starting transfers between devices  25.3 us (10%)
  between operations  14.2 us (5%)
  loops' own time  11.6 us (4%)
  matrix products  9.25 us (4%)
  blocking collectives  7.88 us (3%)
    all_to_all x1, waiting for transfers between devices, shards(): lax.all_to_all(send_rows, 'seq', split_axis=0, concat_axis=0, tiled=True)  45.5 us
    gather x1, other arithmetic, shards(): send_end = jnp.where(usable, frame_ends[clamped], 0).astype(jnp.int32)  40.1 us
    gather x1, other arithmetic, shards(): begins[clamped] < jnp.repeat(frame_high, slot_count)  40 us
    psum x1, waiting for transfers between devices, from_root(): return lax.psum(jnp.where(mine, array, jnp.zeros_like(array)), axis)  23.6 us
    another operation x1, loops' own time, carried_in(): return lax.fori_loop(0, peers, turn, start)  11.6 us
    dynamic_slice x16, local copies, waits for them, and re-layouts, turn(): new = combine(before, everything[k])  10.7 us
    all_to_all x1, starting transfers between devices, shards(): lax.all_to_all(send_end, 'seq', split_axis=0, concat_axis=0, tiled=True)  8.42 us
    unnamed x1, blocking collectives  7.88 us
  transfers between devices with their start and end apart: 5, of which 4 were waited for; matrix products, arithmetic and copies ran while one was open for 7% of the time, Pallas kernels for 0%

commit v1 on v0

v1 whole, which is shorter than its diff:
```python
import functools

import jax
import jax.numpy as jnp
from jax import lax
from jax.experimental import pallas as pl
from jax.experimental.pallas import tpu as pltpu
from jax.sharding import PartitionSpec as P

FR_DEV = 256
COLS = 256
MESH = pl.DeviceIdType.MESH
BF = jnp.bfloat16
F32 = jnp.float32


def factors(seqsize):
    chips = seqsize // 2
    mid = 2 ** ((chips.bit_length() - 1) // 2)
    return chips // mid, mid


def kernel(
    phases, seqsize, slow, mid, rows,
    tokens, weight, gain, unit_weight, unit_gain, durations,
    enc_out, unit_out,
    w_buf, wu_buf, h_in, h_out, h_fin, held, member, total, o_buf, dur_all, durs_buf,
    load_sem, out_sem, relay_send, relay_recv, fin_send, fin_recv,
    dur_send, dur_recv2, dur_recv, up_send, down_send, mid_send, pair_send, recv_sem,
):
    width = tokens.shape[1]
    chunks = width // COLS
    plane = 2 * mid
    p = lax.axis_index("phase")
    s = lax.axis_index("seq")
    z = s // plane
    y = (s // 2) % mid
    c = s % 2
    last = p == phases - 1
    everyone = phases * seqsize
    frames = everyone * FR_DEV
    toks = rows * seqsize
    dmin = frames // (2 * toks)
    dmax = 8 * dmin

    def seq_of(zz, yy, cc):
        return zz * plane + yy * 2 + cc

    def bounds(zz):
        f0 = (p * seqsize + zz * plane) * FR_DEV
        f1 = f0 + plane * FR_DEV - 1
        low = jnp.maximum(f0 // dmax, toks - (frames - f0) // dmin)
        high = jnp.minimum(f1 // dmin, toks - ((frames - f1 - 1) // dmax + 1))
        low = jnp.minimum(low // rows, zz * plane)
        high = jnp.maximum(high // rows, zz * plane + plane - 1)
        return low, high

    low, high = bounds(z)
    low_up, _ = bounds(z + 1)
    _, high_down = bounds(z - 1)

    partners = [(p, seq_of(z, y, 1 - c))]
    partners += [(p, seq_of(z, (y + o) % mid, c)) for o in range(1, mid)]
    partners += [(p, seq_of((z + o) % slow, y, c)) for o in range(1, slow)]
    partners += [((p + o) % phases, s) for o in range(1, phases)]
    barrier = pltpu.get_barrier_semaphore()
    for target in partners:
        pl.semaphore_signal(barrier, inc=1, device_id=target, device_id_type=MESH)
    load_w = pltpu.make_async_copy(weight.at[0], w_buf, load_sem.at[0])
    load_w.start()
    load_wu = pltpu.make_async_copy(unit_weight, wu_buf, load_sem.at[1])
    load_wu.start()

    source = lax.broadcasted_iota(jnp.int32, (rows, 2 * rows), 0)
    lane = lax.broadcasted_iota(jnp.int32, (rows, 2 * rows), 1)
    place = (lane == source + c * rows).astype(BF)
    own = jnp.broadcast_to(durations[...], (8, rows)).astype(F32).astype(BF)
    own = jnp.dot(own, place, preferred_element_type=F32).astype(jnp.int32)
    dur_all[s] = own[0:1, :]

    for b in range(seqsize):
        @pl.when((b < low) | (b > high))
        def _():
            held[b * rows:(b + 1) * rows, :] = jnp.zeros((rows, width), BF)

    pl.semaphore_wait(barrier, len(partners))

    def dur_copy(start, size, sem, recv, target):
        return pltpu.make_async_remote_copy(
            src_ref=dur_all.at[pl.ds(start, size)], dst_ref=dur_all.at[pl.ds(start, size)],
            send_sem=sem, recv_sem=recv, device_id=target, device_id_type=MESH)

    dur_pair = dur_copy(s, 1, dur_send.at[0], dur_recv2.at[0], (p, seq_of(z, y, 1 - c)))
    dur_pair.start()

    def layer_chunks(source_ref, w_ref, gain_row, emit):
        v = source_ref[...].astype(F32)
        scale = lax.rsqrt(jnp.mean(v * v, axis=-1, keepdims=True) + 1e-06)
        normed = (v * gain_row * scale).astype(BF)
        for n in range(chunks):
            part = slice(n * COLS, (n + 1) * COLS)
            x = jnp.dot(normed, w_ref[:, part], preferred_element_type=F32)
            branch = 0.5 * x * (1.0 + jnp.tanh(0.5 * x))
            emit(n, part, (source_ref[:, part].astype(F32) + branch).astype(BF))

    def relay_copy(n):
        part = slice(n * COLS, (n + 1) * COLS)
        return pltpu.make_async_remote_copy(
            src_ref=h_out.at[:, part], dst_ref=h_in.at[:, part],
            send_sem=relay_send.at[n], recv_sem=relay_recv.at[n],
            device_id=((p + 1) % phases, s), device_id_type=MESH)

    def fin_copy(n, o):
        part = slice(n * COLS, (n + 1) * COLS)
        return pltpu.make_async_remote_copy(
            src_ref=h_fin.at[:, part], dst_ref=h_fin.at[:, part],
            send_sem=fin_send.at[n, o - 1], recv_sem=fin_recv.at[n],
            device_id=((p + o) % phases, s), device_id_type=MESH)

    def relay_emit(n, part, value):
        h_out[:, part] = value
        relay_copy(n).start()

    def fin_emit(n, part, value):
        h_fin[:, part] = value
        for o in range(1, phases):
            fin_copy(n, o).start()

    load_w.wait()

    @pl.when(p == 0)
    def _():
        layer_chunks(tokens, w_buf, gain[...], relay_emit if phases > 1 else fin_emit)

    dur_pair.wait()
    mids = [dur_copy(seq_of(z, y, 0), 2, dur_send.at[o], dur_recv2.at[o],
                     (p, seq_of(z, (y + o) % mid, c))) for o in range(1, mid)]
    for copy in mids:
        copy.start()
    for copy in mids:
        copy.wait()
    slows = [dur_copy(z * plane, plane, dur_send.at[mid - 1 + o], dur_recv.at[o],
                      (p, seq_of((z + o) % slow, y, c))) for o in range(1, slow)]
    for copy in slows:
        copy.start()
    for copy in slows:
        copy.wait()
    pairs = seqsize // 2
    for q in range(pairs):
        durs_buf[q:q + 1, :] = (dur_all[2 * q] + dur_all[2 * q + 1]).astype(F32)
    durs = durs_buf[...]
    tri = (lax.broadcasted_iota(jnp.int32, (2 * rows, 2 * rows), 0)
           <= lax.broadcasted_iota(jnp.int32, (2 * rows, 2 * rows), 1)).astype(BF)
    inner = jnp.dot(durs.astype(BF), tri, preferred_element_type=F32)
    frame = (lax.broadcasted_iota(jnp.int32, (FR_DEV, 2 * rows), 0)
             + (p * seqsize + s) * FR_DEV).astype(F32)
    before = jnp.zeros((1, 1), F32)
    for q in range(pairs):
        ends = inner[q:q + 1, :] + before
        begins = ends - durs[q:q + 1, :]
        inside = jnp.where((frame >= begins) & (frame < ends), 1.0, 0.0).astype(BF)
        at = (q % mid) * 2 * rows
        member[q // mid, :, at:at + 2 * rows] = inside
        before = before + jnp.sum(durs[q:q + 1, :], axis=1, keepdims=True)

    if phases > 1:
        @pl.when(p > 0)
        def _():
            for n in range(chunks):
                relay_copy(n).wait_recv()

            @pl.when(jnp.logical_not(last))
            def _():
                layer_chunks(h_in, w_buf, gain[...], relay_emit)

            @pl.when(last)
            def _():
                layer_chunks(h_in, w_buf, gain[...], fin_emit)

        @pl.when(jnp.logical_not(last))
        def _():
            for n in range(chunks):
                fin_copy(n, 1).wait_recv()

    enc_copy = pltpu.make_async_copy(h_fin, enc_out, out_sem.at[0])
    enc_copy.start()

    def block(b):
        return held.at[pl.ds(pl.multiple_of(b * rows, rows), rows)]

    def send(b, sem, target):
        return pltpu.make_async_remote_copy(
            src_ref=block(b), dst_ref=block(b), send_sem=sem, recv_sem=recv_sem.at[b],
            device_id=target, device_id_type=MESH)

    def up(zz):
        return send(seq_of(zz, y, c), up_send.at[zz], (p, seq_of((z + 1) % slow, y, c)))

    def down(zz):
        return send(seq_of(zz, y, c), down_send.at[zz], (p, seq_of((z + slow - 1) % slow, y, c)))

    def across(zz, o):
        return send(seq_of(zz, y, c), mid_send.at[zz, o], (p, seq_of(z, (y + o) % mid, c)))

    def sibling(b):
        return send(b, pair_send.at[b], (p, seq_of(z, y, 1 - c)))

    def goes_up(zz):
        return (z + 1 < slow) & (zz <= z) & (seq_of(zz, y, c) >= low_up)

    def goes_down(zz):
        return (z > 0) & (zz >= z) & (seq_of(zz, y, c) <= high_down)

    def wanted(b):
        return (b >= low) & (b <= high)

    load_wu.wait()

    def unit_emit(n, part, value):
        held[pl.ds(pl.multiple_of(s * rows, rows), rows), part] = value

    layer_chunks(h_fin, wu_buf, unit_gain[...], unit_emit)

    def spread_column(zz):
        @pl.when(goes_up(zz))
        def _():
            up(zz).start()

        @pl.when(goes_down(zz))
        def _():
            down(zz).start()

        for o in range(1, mid):
            across(zz, o).start()
        sibling(seq_of(zz, y, c)).start()

    def valid(zz):
        return (zz >= 0) & (zz < slow)

    def column(zz):
        @pl.when(valid(zz) & wanted(seq_of(zz, y, c)))
        def _():
            b = seq_of(zz, y, c)
            send(b, pair_send.at[b], (p, s)).wait_recv()
            spread_column(zz)

    def from_across(zz):
        for o in range(1, mid):
            b = seq_of(zz, (y + o) % mid, c)

            @pl.when(valid(zz) & wanted(b))
            def _():
                send(b, pair_send.at[b], (p, s)).wait_recv()
                sibling(b).start()

    def add_plane(zz, first):
        def work():
            for yy in range(mid):
                b = seq_of(zz, yy, 1 - c)

                @pl.when(wanted(b))
                def _():
                    send(b, pair_send.at[b], (p, s)).wait_recv()

            mask = member[zz]

            def one(n, carry):
                cols = pl.ds(pl.multiple_of(n * COLS, COLS), COLS)
                rows_at = pl.ds(pl.multiple_of(zz * plane * rows, plane * rows), plane * rows)
                got = jnp.dot(mask, held[rows_at, cols], preferred_element_type=F32)
                if first:
                    total[:, cols] = got
                else:
                    total[:, cols] += got
                return carry

            lax.fori_loop(0, chunks, one, 0)

        if first:
            work()
        else:
            pl.when(valid(zz) & (zz * plane + plane - 1 >= low) & (zz * plane <= high))(work)

    spread_column(z)
    for k in range(1, slow + 1):
        if k < slow:
            column(z - k)
            column(z + k)
        if k == 1:
            from_across(z)
            add_plane(z, True)
        else:
            for zz in (z - k + 1, z + k - 1):
                from_across(zz)
                add_plane(zz, False)

    out_copies = []
    part_rows = FR_DEV // 4
    for r in range(4):
        part = slice(r * part_rows, (r + 1) * part_rows)
        o_buf[part, :] = total[part, :].astype(BF)
        copy = pltpu.make_async_copy(o_buf.at[part], unit_out.at[part], out_sem.at[1 + r])
        copy.start()
        out_copies.append(copy)

    if phases > 1:
        @pl.when(jnp.logical_not(last))
        def _():
            for n in range(chunks):
                relay_copy(n).wait_send()

        @pl.when(last)
        def _():
            for n in range(chunks):
                for o in range(1, phases):
                    fin_copy(n, o).wait_send()

    for zz in range(slow):
        @pl.when(wanted(seq_of(zz, y, c)))
        def _():
            @pl.when(goes_up(zz))
            def _():
                up(zz).wait_send()

            @pl.when(goes_down(zz))
            def _():
                down(zz).wait_send()

            for o in range(1, mid):
                across(zz, o).wait_send()

        for yy in range(mid):
            b = seq_of(zz, yy, c)

            @pl.when(wanted(b))
            def _():
                sibling(b).wait_send()

    enc_copy.wait()
    for copy in out_copies:
        copy.wait()


def shards(tokens, phase_weight, phase_gain, unit_weight, unit_gain, durations):
    phases = lax.axis_size("phase")
    seqsize = lax.axis_size("seq")
    slow, mid = factors(seqsize)
    rows, width = tokens.shape
    chunks = width // COLS
    vmem = pl.BlockSpec(memory_space=pltpu.VMEM)
    anywhere = pl.BlockSpec(memory_space=pl.ANY)
    dma = pltpu.SemaphoreType.DMA
    return pl.pallas_call(
        functools.partial(kernel, phases, seqsize, slow, mid, rows),
        out_shape=(
            jax.ShapeDtypeStruct((rows, width), BF),
            jax.ShapeDtypeStruct((FR_DEV, width), BF),
        ),
        in_specs=[vmem, anywhere, vmem, anywhere, vmem, vmem],
        out_specs=(anywhere, anywhere),
        scratch_shapes=[
            pltpu.VMEM((width, width), BF),
            pltpu.VMEM((width, width), BF),
            pltpu.VMEM((rows, width), BF),
            pltpu.VMEM((rows, width), BF),
            pltpu.VMEM((rows, width), BF),
            pltpu.VMEM((rows * seqsize, width), BF),
            pltpu.VMEM((slow, FR_DEV, 2 * mid * rows), BF),
            pltpu.VMEM((FR_DEV, width), F32),
            pltpu.VMEM((FR_DEV, width), BF),
            pltpu.VMEM((seqsize, 1, 2 * rows), jnp.int32),
            pltpu.VMEM((seqsize // 2, 2 * rows), F32),
            dma((2,)),
            dma((5,)),
            dma((chunks,)),
            dma((chunks,)),
            dma((chunks, max(phases - 1, 1))),
            dma((chunks,)),
            dma((mid + slow,)),
            dma((mid,)),
            dma((slow,)),
            dma((slow,)),
            dma((slow,)),
            dma((slow, mid)),
            dma((seqsize,)),
            dma((seqsize,)),
        ],
        compiler_params=pltpu.CompilerParams(
            collective_id=0, has_side_effects=True, vmem_limit_bytes=40 * 1024 * 1024
        ),
        cost_estimate=pl.CostEstimate(
            flops=10 ** 9, bytes_accessed=8 * 10 ** 6, transcendentals=2 * 10 ** 5
        ),
    )(tokens, phase_weight, phase_gain, unit_weight, unit_gain.reshape(1, width),
      durations.reshape(1, rows))


def solution(mesh):
    return jax.shard_map(
        shards,
        mesh=mesh,
        in_specs=(P("seq", None), P("phase", None, None), P("phase", None), P(), P(), P("seq")),
        out_specs=(P("seq", None), P(("phase", "seq"), None)),
        check_vma=False,
    )
```

time: 259 us -> 43.2 us (0.17)
  the two profiles are of different devices: /device:TPU:13 before, /device:TPU:25 now
where the time goes in v1:
time: 43.2 us; the launch traced here: 42.9 us
  Pallas kernels  34.7 us (80%)
  local copies, waits for them, and re-layouts  7.56 us (18%)
  between operations  0.65 us (2%)
    pallas_call x1, Pallas kernels, shards(): pl.pallas_call(functools.partial(kernel, phases, seqsize, slow, mid, rows...  34.7 us
    unnamed x14, local copies, waits for them, and re-layouts  7.56 us

profile of v1, /device:TPU:25, one launch (start us, length us, event | category | flops | bytes accessed | tf_op | source)
XLA Modules:
  0.0 42.9 jit_solution(1713123360979533853)
XLA Ops:
  0.6 0.0 copy-start
  0.6 1.6 %copy-done = bf16[1,1024,1024]{2,1,0:T(8,128)(2,1)S(1)} copy-done((bf16[1,1024,1024]{2,1,0:T(8,128)(2,1)S(1)}, bf16[1,1024,1024]{2,1,0:T(8,128)(2,1)}, u32[]{:S(2)}) %copy-start) | copy-done | bytes 2097176
  2.2 0.0 copy-start.1
  2.2 1.6 %copy-done.1 = bf16[1024,1024]{1,0:T(8,128)(2,1)S(1)} copy-done((bf16[1024,1024]{1,0:T(8,128)(2,1)S(1)}, bf16[1024,1024]{1,0:T(8,128)(2,1)}, u32[]{:S(2)}) %copy-start.1) | copy-done | bytes 2097176
  3.8 0.0 copy-start.2
  3.8 0.9 %copy-done.2 = bf16[64,1024]{1,0:T(8,128)(2,1)S(1)} copy-done((bf16[64,1024]{1,0:T(8,128)(2,1)S(1)}, bf16[64,1024]{1,0:T(8,128)(2,1)}, u32[]{:S(2)}) %copy-start.2) | copy-done | bytes 131096
  4.7 0.0 copy-start.3
  4.7 0.7 %copy-done.3 = f32[1,1024]{1,0:T(1,128)S(1)} copy-done((f32[1,1024]{1,0:T(1,128)S(1)}, f32[1,1024]{1,0:T(1,128)}, u32[]{:S(2)}) %copy-start.3) | copy-done | bytes 4120
  5.4 0.0 copy-start.4
  5.4 0.7 %copy-done.4 = f32[1024]{0:T(1024)S(1)} copy-done((f32[1024]{0:T(1024)S(1)}, f32[1024]{0:T(1024)}, u32[]{:S(2)}) %copy-start.4) | copy-done | bytes 4120
  6.1 0.0 copy-start.5
  6.1 0.7 %copy-done.5 = s32[64]{0:T(128)S(1)} copy-done((s32[64]{0:T(128)S(1)}, s32[64]{0:T(128)}, u32[]{:S(2)}) %copy-start.5) | copy-done | bytes 280
  6.8 34.7 %shard_map.77 = (bf16[64,1024]{1,0:T(8,128)(2,1)S(1)}, bf16[256,1024]{1,0:T(8,128)(2,1)S(1)}) custom-call(bf16[64,1024]{1,0:T(8,128)(2,1)S(1)} %copy-done.2, bf16[1,1024,1024]{2,1,0:T(8,128)(2,1)S(1)} %copy-done, f32[1,1024]{1,0:T(1,128)S(1)} %copy-done.3, bf16[1024,1024]{1,0:T(8,128)(2,1)S(1)} %copy-done.1, f32[1,1024]{1,0:T(1,128)S(1)} %bitcast.2, ...), custom_call_target="tpu_custom_call" | custom-call | flops 1000000000 | bytes 8000000 | tf_op jit(solution)/shard_map/pallas_call | solution.py:353
  41.4 0.7 %copy.10 = bf16[64,1024]{1,0:T(8,128)(2,1)} copy(bf16[64,1024]{1,0:T(8,128)(2,1)S(1)} %get-tuple-element.4) | data formatting | bytes 262144
  42.1 0.8 %copy.11 = bf16[256,1024]{1,0:T(8,128)(2,1)} copy(bf16[256,1024]{1,0:T(8,128)(2,1)S(1)} %get-tuple-element.5) | data formatting | bytes 1048576
Async XLA Ops:
  0.6 1.6 %copy-start = (bf16[1,1024,1024]{2,1,0:T(8,128)(2,1)S(1)}, bf16[1,1024,1024]{2,1,0:T(8,128)(2,1)}, u32[]{:S(2)}) copy-start(bf16[1,1024,1024]{2,1,0:T(8,128)(2,1)} %weight.1) | copy-start | bytes 6291460
  2.2 1.6 %copy-start.1 = (bf16[1024,1024]{1,0:T(8,128)(2,1)S(1)}, bf16[1024,1024]{1,0:T(8,128)(2,1)}, u32[]{:S(2)}) copy-start(bf16[1024,1024]{1,0:T(8,128)(2,1)} %unit_weight.1) | copy-start | bytes 6291460
  3.8 0.9 %copy-start.2 = (bf16[64,1024]{1,0:T(8,128)(2,1)S(1)}, bf16[64,1024]{1,0:T(8,128)(2,1)}, u32[]{:S(2)}) copy-start(bf16[64,1024]{1,0:T(8,128)(2,1)} %tokens.1) | copy-start | bytes 393220
  4.7 0.7 %copy-start.3 = (f32[1,1024]{1,0:T(1,128)S(1)}, f32[1,1024]{1,0:T(1,128)}, u32[]{:S(2)}) copy-start(f32[1,1024]{1,0:T(1,128)} %gain.1) | copy-start | bytes 12292
  5.4 0.7 %copy-start.4 = (f32[1024]{0:T(1024)S(1)}, f32[1024]{0:T(1024)}, u32[]{:S(2)}) copy-start(f32[1024]{0:T(1024)} %param.10) | copy-start | bytes 12292
  6.1 0.7 %copy-start.5 = (s32[64]{0:T(128)S(1)}, s32[64]{0:T(128)}, u32[]{:S(2)}) copy-start(s32[64]{0:T(128)} %param.11) | copy-start | bytes 772

commit v2 on v1

--- a/solution.py
+++ b/solution.py
@@ -22,11 +22,11 @@
 
 def kernel(
     phases, seqsize, slow, mid, rows,
-    tokens, weight, gain, unit_weight, unit_gain, durations,
+    tokens_hbm, weight, gain_hbm, unit_weight, unit_gain_hbm, durations_hbm,
     enc_out, unit_out,
-    w_buf, wu_buf, h_in, h_out, h_fin, held, member, total, o_buf, dur_all, durs_buf,
+    tokens, gain, unit_gain, durations, w_buf, wu_buf, h_in, h_out, h_fin, held, member, total, o_buf, dur_all, durs_buf,
     load_sem, out_sem, relay_send, relay_recv, fin_send, fin_recv,
-    dur_send, dur_recv2, dur_recv, up_send, down_send, mid_send, pair_send, recv_sem,
+    dur_send, dur_near, dur_recv, up_send, down_send, mid_send, pair_send, recv_sem,
 ):
     width = tokens.shape[1]
     chunks = width // COLS
@@ -60,17 +60,26 @@
     _, high_down = bounds(z - 1)
 
     partners = [(p, seq_of(z, y, 1 - c))]
-    partners += [(p, seq_of(z, (y + o) % mid, c)) for o in range(1, mid)]
+    partners += [(p, seq_of(z, (y + o) % mid, cc)) for o in range(1, mid) for cc in (c, 1 - c)]
     partners += [(p, seq_of((z + o) % slow, y, c)) for o in range(1, slow)]
     partners += [((p + o) % phases, s) for o in range(1, phases)]
     barrier = pltpu.get_barrier_semaphore()
     for target in partners:
         pl.semaphore_signal(barrier, inc=1, device_id=target, device_id_type=MESH)
+    loads = [
+        pltpu.make_async_copy(source, target, load_sem.at[2 + i])
+        for i, (source, target) in enumerate([
+            (durations_hbm, durations), (tokens_hbm, tokens), (gain_hbm, gain),
+            (unit_gain_hbm, unit_gain)])
+    ]
+    for load in loads:
+        load.start()
     load_w = pltpu.make_async_copy(weight.at[0], w_buf, load_sem.at[0])
     load_w.start()
     load_wu = pltpu.make_async_copy(unit_weight, wu_buf, load_sem.at[1])
     load_wu.start()
 
+    loads[0].wait()
     source = lax.broadcasted_iota(jnp.int32, (rows, 2 * rows), 0)
     lane = lax.broadcasted_iota(jnp.int32, (rows, 2 * rows), 1)
     place = (lane == source + c * rows).astype(BF)
@@ -90,8 +99,12 @@
             src_ref=dur_all.at[pl.ds(start, size)], dst_ref=dur_all.at[pl.ds(start, size)],
             send_sem=sem, recv_sem=recv, device_id=target, device_id_type=MESH)
 
-    dur_pair = dur_copy(s, 1, dur_send.at[0], dur_recv2.at[0], (p, seq_of(z, y, 1 - c)))
-    dur_pair.start()
+    def near(i):
+        return dur_copy(s, 1, dur_send.at[i], dur_near.at[i], (p, seq_of(
+            z, (y + (i + 1) // 2) % mid, (c + i + 1) % 2)))
+
+    for i in range(plane - 1):
+        near(i).start()
 
     def layer_chunks(source_ref, w_ref, gain_row, emit):
         v = source_ref[...].astype(F32)
@@ -126,42 +139,45 @@
         for o in range(1, phases):
             fin_copy(n, o).start()
 
+    for load in loads[1:]:
+        load.wait()
     load_w.wait()
 
     @pl.when(p == 0)
     def _():
         layer_chunks(tokens, w_buf, gain[...], relay_emit if phases > 1 else fin_emit)
 
-    dur_pair.wait()
-    mids = [dur_copy(seq_of(z, y, 0), 2, dur_send.at[o], dur_recv2.at[o],
-                     (p, seq_of(z, (y + o) % mid, c))) for o in range(1, mid)]
-    for copy in mids:
-        copy.start()
-    for copy in mids:
-        copy.wait()
-    slows = [dur_copy(z * plane, plane, dur_send.at[mid - 1 + o], dur_recv.at[o],
-                      (p, seq_of((z + o) % slow, y, c))) for o in range(1, slow)]
-    for copy in slows:
-        copy.start()
-    for copy in slows:
-        copy.wait()
-    pairs = seqsize // 2
-    for q in range(pairs):
-        durs_buf[q:q + 1, :] = (dur_all[2 * q] + dur_all[2 * q + 1]).astype(F32)
-    durs = durs_buf[...]
-    tri = (lax.broadcasted_iota(jnp.int32, (2 * rows, 2 * rows), 0)
-           <= lax.broadcasted_iota(jnp.int32, (2 * rows, 2 * rows), 1)).astype(BF)
-    inner = jnp.dot(durs.astype(BF), tri, preferred_element_type=F32)
-    frame = (lax.broadcasted_iota(jnp.int32, (FR_DEV, 2 * rows), 0)
-             + (p * seqsize + s) * FR_DEV).astype(F32)
-    before = jnp.zeros((1, 1), F32)
-    for q in range(pairs):
-        ends = inner[q:q + 1, :] + before
-        begins = ends - durs[q:q + 1, :]
-        inside = jnp.where((frame >= begins) & (frame < ends), 1.0, 0.0).astype(BF)
-        at = (q % mid) * 2 * rows
-        member[q // mid, :, at:at + 2 * rows] = inside
-        before = before + jnp.sum(durs[q:q + 1, :], axis=1, keepdims=True)
+    def far(o):
+        return dur_copy(z * plane, plane, dur_send.at[plane - 1 + o], dur_recv.at[o],
+                        (p, seq_of((z + o) % slow, y, c)))
+
+    for i in range(plane - 1):
+        near(i).wait()
+    for o in range(1, slow):
+        far(o).start()
+
+    def make_member():
+        for o in range(1, slow):
+            far(o).wait()
+        pairs = seqsize // 2
+        for q in range(pairs):
+            durs_buf[q:q + 1, :] = (dur_all[2 * q] + dur_all[2 * q + 1]).astype(F32)
+        durs = durs_buf[...]
+        tri = (lax.broadcasted_iota(jnp.int32, (2 * rows, 2 * rows), 0)
+               <= lax.broadcasted_iota(jnp.int32, (2 * rows, 2 * rows), 1)).astype(BF)
+        inner = jnp.dot(durs.astype(BF), tri, preferred_element_type=F32)
+        frame = (lax.broadcasted_iota(jnp.int32, (FR_DEV, 2 * rows), 0)
+                 + (p * seqsize + s) * FR_DEV).astype(F32)
+        before = jnp.zeros((1, 1), F32)
+        for q in range(pairs):
+            ends = inner[q:q + 1, :] + before
+            begins = ends - durs[q:q + 1, :]
+            inside = jnp.where((frame >= begins) & (frame < ends), 1.0, 0.0).astype(BF)
+            at = (q % mid) * 2 * rows
+            member[q // mid, :, at:at + 2 * rows] = inside
+            before = before + jnp.sum(durs[q:q + 1, :], axis=1, keepdims=True)
+
+    pl.when(jnp.logical_not(last))(make_member)
 
     if phases > 1:
         @pl.when(p > 0)
@@ -282,6 +298,7 @@
             pl.when(valid(zz) & (zz * plane + plane - 1 >= low) & (zz * plane <= high))(work)
 
     spread_column(z)
+    pl.when(last)(make_member)
     for k in range(1, slow + 1):
         if k < slow:
             column(z - k)
@@ -347,8 +364,8 @@
     slow, mid = factors(seqsize)
     rows, width = tokens.shape
     chunks = width // COLS
-    vmem = pl.BlockSpec(memory_space=pltpu.VMEM)
     anywhere = pl.BlockSpec(memory_space=pl.ANY)
+    hbm = pl.BlockSpec(memory_space=pltpu.HBM)
     dma = pltpu.SemaphoreType.DMA
     return pl.pallas_call(
         functools.partial(kernel, phases, seqsize, slow, mid, rows),
@@ -356,9 +373,13 @@
             jax.ShapeDtypeStruct((rows, width), BF),
             jax.ShapeDtypeStruct((FR_DEV, width), BF),
         ),
-        in_specs=[vmem, anywhere, vmem, anywhere, vmem, vmem],
+        in_specs=[hbm] * 6,
         out_specs=(anywhere, anywhere),
         scratch_shapes=[
+            pltpu.VMEM((rows, width), BF),
+            pltpu.VMEM((1, width), F32),
+            pltpu.VMEM((1, width), F32),
+            pltpu.VMEM((1, rows), jnp.int32),
             pltpu.VMEM((width, width), BF),
             pltpu.VMEM((width, width), BF),
             pltpu.VMEM((rows, width), BF),
@@ -370,14 +391,14 @@
             pltpu.VMEM((FR_DEV, width), BF),
             pltpu.VMEM((seqsize, 1, 2 * rows), jnp.int32),
             pltpu.VMEM((seqsize // 2, 2 * rows), F32),
-            dma((2,)),
+            dma((6,)),
             dma((5,)),
             dma((chunks,)),
             dma((chunks,)),
             dma((chunks, max(phases - 1, 1))),
             dma((chunks,)),
-            dma((mid + slow,)),
-            dma((mid,)),
+            dma((2 * mid + slow,)),
+            dma((2 * mid,)),
             dma((slow,)),
             dma((slow,)),
             dma((slow,)),
@@ -386,7 +407,7 @@
             dma((seqsize,)),
         ],
         compiler_params=pltpu.CompilerParams(
-            collective_id=0, has_side_effects=True, vmem_limit_bytes=40 * 1024 * 1024
+            collective_id=0, has_side_effects=True, vmem_limit_bytes=63 * 1024 * 1024
         ),
         cost_estimate=pl.CostEstimate(
             flops=10 ** 9, bytes_accessed=8 * 10 ** 6, transcendentals=2 * 10 ** 5

time: 43.2 us -> 36 us (0.83)
  local copies, waits for them, and re-layouts: 7.56 us -> 3.44 us
  Pallas kernels: 34.7 us -> 31.7 us
    unnamed x14 -> x2, local copies, waits for them, and re-layouts: 7.56 us -> 3.44 us
    pallas_call x1, Pallas kernels: 34.7 us -> 31.7 us  [shards(): pl.pallas_call(functools.partial(kernel, phases, seqsize, slow, mid, rows...]
where the time goes in v2:
time: 36 us; the launch traced here: 35.8 us
  Pallas kernels  31.7 us (88%)
  local copies, waits for them, and re-layouts  3.44 us (10%)
  between operations  0.64 us (2%)
    pallas_call x1, Pallas kernels, shards(): pl.pallas_call(functools.partial(kernel, phases, seqsize, slow, mid, rows...  31.7 us
    unnamed x2, local copies, waits for them, and re-layouts  3.44 us

profile of v2, /device:TPU:25, one launch (start us, length us, event | category | flops | bytes accessed | tf_op | source)
XLA Modules:
  0.0 35.8 jit_solution(6835850390396818848)
XLA Ops:
  0.6 31.7 %shard_map.77 = (bf16[64,1024]{1,0:T(8,128)(2,1)}, bf16[256,1024]{1,0:T(8,128)(2,1)}) custom-call(bf16[64,1024]{1,0:T(8,128)(2,1)} %tokens_hbm.1, bf16[1,1024,1024]{2,1,0:T(8,128)(2,1)} %weight.1, f32[1,1024]{1,0:T(1,128)} %gain_hbm.1, bf16[1024,1024]{1,0:T(8,128)(2,1)} %unit_weight.1, f32[1,1024]{1,0:T(1,128)} %bitcast.2, s32[1,64]{1,0:T(1,128)} %bitcast.3), custom_call_target="tpu_custom_call" | custom-call | flops 1000000000 | bytes 8000000 | tf_op jit(solution)/shard_map/pallas_call | solution.py:370
  32.4 1.6 %copy.10 = bf16[64,1024]{1,0:T(8,128)(2,1)} copy(bf16[64,1024]{1,0:T(8,128)(2,1)} %get-tuple-element.4) | data formatting | bytes 262144
  33.9 1.9 %copy.11 = bf16[256,1024]{1,0:T(8,128)(2,1)} copy(bf16[256,1024]{1,0:T(8,128)(2,1)} %get-tuple-element.5) | data formatting | bytes 1048576

commit v3 on v2

--- a/solution.py
+++ b/solution.py
@@ -9,6 +9,7 @@
 
 FR_DEV = 256
 COLS = 256
+HALVES = 2
 MESH = pl.DeviceIdType.MESH
 BF = jnp.bfloat16
 F32 = jnp.float32
@@ -77,7 +78,6 @@
     load_w = pltpu.make_async_copy(weight.at[0], w_buf, load_sem.at[0])
     load_w.start()
     load_wu = pltpu.make_async_copy(unit_weight, wu_buf, load_sem.at[1])
-    load_wu.start()
 
     loads[0].wait()
     source = lax.broadcasted_iota(jnp.int32, (rows, 2 * rows), 0)
@@ -142,6 +142,7 @@
     for load in loads[1:]:
         load.wait()
     load_w.wait()
+    load_wu.start()
 
     @pl.when(p == 0)
     def _():
@@ -201,25 +202,31 @@
     enc_copy = pltpu.make_async_copy(h_fin, enc_out, out_sem.at[0])
     enc_copy.start()
 
-    def block(b):
-        return held.at[pl.ds(pl.multiple_of(b * rows, rows), rows)]
-
-    def send(b, sem, target):
+    half = width // HALVES
+
+    def block(b, h):
+        return held.at[pl.ds(pl.multiple_of(b * rows, rows), rows), h * half:(h + 1) * half]
+
+    def send(b, h, sem, target):
         return pltpu.make_async_remote_copy(
-            src_ref=block(b), dst_ref=block(b), send_sem=sem, recv_sem=recv_sem.at[b],
+            src_ref=block(b, h), dst_ref=block(b, h), send_sem=sem, recv_sem=recv_sem.at[b, h],
             device_id=target, device_id_type=MESH)
 
-    def up(zz):
-        return send(seq_of(zz, y, c), up_send.at[zz], (p, seq_of((z + 1) % slow, y, c)))
-
-    def down(zz):
-        return send(seq_of(zz, y, c), down_send.at[zz], (p, seq_of((z + slow - 1) % slow, y, c)))
-
-    def across(zz, o):
-        return send(seq_of(zz, y, c), mid_send.at[zz, o], (p, seq_of(z, (y + o) % mid, c)))
-
-    def sibling(b):
-        return send(b, pair_send.at[b], (p, seq_of(z, y, 1 - c)))
+    def up(zz, h):
+        return send(seq_of(zz, y, c), h, up_send.at[zz, h], (p, seq_of((z + 1) % slow, y, c)))
+
+    def down(zz, h):
+        return send(seq_of(zz, y, c), h, down_send.at[zz, h],
+                    (p, seq_of((z + slow - 1) % slow, y, c)))
+
+    def across(zz, o, h):
+        return send(seq_of(zz, y, c), h, mid_send.at[zz, o, h], (p, seq_of(z, (y + o) % mid, c)))
+
+    def sibling(b, h):
+        return send(b, h, pair_send.at[b, h], (p, seq_of(z, y, 1 - c)))
+
+    def arrived(b, h):
+        sibling(b, h).wait_recv()
 
     def goes_up(zz):
         return (z + 1 < slow) & (zz <= z) & (seq_of(zz, y, c) >= low_up)
@@ -230,95 +237,98 @@
     def wanted(b):
         return (b >= low) & (b <= high)
 
+    def valid(zz):
+        return (zz >= 0) & (zz < slow)
+
+    def spread_column(zz, h):
+        @pl.when(goes_up(zz))
+        def _():
+            up(zz, h).start()
+
+        @pl.when(goes_down(zz))
+        def _():
+            down(zz, h).start()
+
+        for o in range(1, mid):
+            across(zz, o, h).start()
+        sibling(seq_of(zz, y, c), h).start()
+
     load_wu.wait()
 
     def unit_emit(n, part, value):
         held[pl.ds(pl.multiple_of(s * rows, rows), rows), part] = value
+        if (n + 1) * COLS % half == 0:
+            spread_column(z, n * COLS // half)
 
     layer_chunks(h_fin, wu_buf, unit_gain[...], unit_emit)
 
-    def spread_column(zz):
-        @pl.when(goes_up(zz))
-        def _():
-            up(zz).start()
-
-        @pl.when(goes_down(zz))
-        def _():
-            down(zz).start()
-
-        for o in range(1, mid):
-            across(zz, o).start()
-        sibling(seq_of(zz, y, c)).start()
-
-    def valid(zz):
-        return (zz >= 0) & (zz < slow)
-
-    def column(zz):
-        @pl.when(valid(zz) & wanted(seq_of(zz, y, c)))
-        def _():
-            b = seq_of(zz, y, c)
-            send(b, pair_send.at[b], (p, s)).wait_recv()
-            spread_column(zz)
-
-    def from_across(zz):
+    def column(zz, h):
+        b = seq_of(zz, y, c)
+
+        @pl.when(valid(zz) & wanted(b))
+        def _():
+            arrived(b, h)
+            spread_column(zz, h)
+
+    def from_across(zz, h):
         for o in range(1, mid):
             b = seq_of(zz, (y + o) % mid, c)
 
             @pl.when(valid(zz) & wanted(b))
             def _():
-                send(b, pair_send.at[b], (p, s)).wait_recv()
-                sibling(b).start()
-
-    def add_plane(zz, first):
+                arrived(b, h)
+                sibling(b, h).start()
+
+    def add_plane(zz, h, first):
         def work():
             for yy in range(mid):
                 b = seq_of(zz, yy, 1 - c)
 
                 @pl.when(wanted(b))
                 def _():
-                    send(b, pair_send.at[b], (p, s)).wait_recv()
+                    arrived(b, h)
 
             mask = member[zz]
-
-            def one(n, carry):
-                cols = pl.ds(pl.multiple_of(n * COLS, COLS), COLS)
-                rows_at = pl.ds(pl.multiple_of(zz * plane * rows, plane * rows), plane * rows)
+            rows_at = pl.ds(pl.multiple_of(zz * plane * rows, plane * rows), plane * rows)
+            for n in range(h * half // COLS, (h + 1) * half // COLS):
+                cols = slice(n * COLS, (n + 1) * COLS)
                 got = jnp.dot(mask, held[rows_at, cols], preferred_element_type=F32)
                 if first:
                     total[:, cols] = got
                 else:
                     total[:, cols] += got
-                return carry
-
-            lax.fori_loop(0, chunks, one, 0)
 
         if first:
             work()
         else:
             pl.when(valid(zz) & (zz * plane + plane - 1 >= low) & (zz * plane <= high))(work)
 
-    spread_column(z)
     pl.when(last)(make_member)
-    for k in range(1, slow + 1):
-        if k < slow:
-            column(z - k)
-            column(z + k)
-        if k == 1:
-            from_across(z)
-            add_plane(z, True)
-        else:
-            for zz in (z - k + 1, z + k - 1):
-                from_across(zz)
-                add_plane(zz, False)
-
     out_copies = []
-    part_rows = FR_DEV // 4
-    for r in range(4):
-        part = slice(r * part_rows, (r + 1) * part_rows)
-        o_buf[part, :] = total[part, :].astype(BF)
-        copy = pltpu.make_async_copy(o_buf.at[part], unit_out.at[part], out_sem.at[1 + r])
-        copy.start()
-        out_copies.append(copy)
+    steps = [(k, h) for k in range(slow) for h in range(HALVES)]
+    for i in range(HALVES, len(steps) + 4):
+        if i < len(steps):
+            k, h = steps[i]
+            column(z - k, h)
+            column(z + k, h)
+        if i == HALVES:
+            for h in range(HALVES - 1):
+                from_across(z, h)
+        if i - 1 < len(steps):
+            k, h = steps[i - 1]
+            for zz in (z - k, z + k) if k else (z,):
+                from_across(zz, h)
+        if 0 <= i - 4 < len(steps):
+            k, h = steps[i - 4]
+            for zz in (z - k, z + k) if k else (z,):
+                add_plane(zz, h, k == 0)
+            if k == slow - 1:
+                part = slice(h * half, (h + 1) * half)
+                o_buf[:, part] = total[:, part].astype(BF)
+                copy = pltpu.make_async_copy(o_buf.at[:, part], unit_out.at[:, part],
+                                             out_sem.at[1 + h])
+                copy.start()
+                out_copies.append(copy)
 
     if phases > 1:
         @pl.when(jnp.logical_not(last))
@@ -335,23 +345,25 @@
     for zz in range(slow):
         @pl.when(wanted(seq_of(zz, y, c)))
         def _():
-            @pl.when(goes_up(zz))
-            def _():
-                up(zz).wait_send()
-
-            @pl.when(goes_down(zz))
-            def _():
-                down(zz).wait_send()
-
-            for o in range(1, mid):
-                across(zz, o).wait_send()
+            for h in range(HALVES):
+                @pl.when(goes_up(zz))
+                def _():
+                    up(zz, h).wait_send()
+
+                @pl.when(goes_down(zz))
+                def _():
+                    down(zz, h).wait_send()
+
+                for o in range(1, mid):
+                    across(zz, o, h).wait_send()
 
         for yy in range(mid):
             b = seq_of(zz, yy, c)
 
             @pl.when(wanted(b))
             def _():
-                sibling(b).wait_send()
+                for h in range(HALVES):
+                    sibling(b, h).wait_send()
 
     enc_copy.wait()
     for copy in out_copies:
@@ -370,8 +382,8 @@
     return pl.pallas_call(
         functools.partial(kernel, phases, seqsize, slow, mid, rows),
         out_shape=(
-            jax.ShapeDtypeStruct((rows, width), BF),
-            jax.ShapeDtypeStruct((FR_DEV, width), BF),
+            pltpu.VMEM((rows, width), BF),
+            pltpu.VMEM((FR_DEV, width), BF),
         ),
         in_specs=[hbm] * 6,
         out_specs=(anywhere, anywhere),
@@ -400,20 +412,20 @@
             dma((2 * mid + slow,)),
             dma((2 * mid,)),
             dma((slow,)),
-            dma((slow,)),
-            dma((slow,)),
-            dma((slow, mid)),
-            dma((seqsize,)),
-            dma((seqsize,)),
+            dma((slow, HALVES)),
+            dma((slow, HALVES)),
+            dma((slow, mid, HALVES)),
+            dma((seqsize, HALVES)),
+            dma((seqsize, HALVES)),
         ],
         compiler_params=pltpu.CompilerParams(
-            collective_id=0, has_side_effects=True, vmem_limit_bytes=63 * 1024 * 1024
+            collective_id=0, has_side_effects=True, vmem_limit_bytes=40 * 1024 * 1024
         ),
         cost_estimate=pl.CostEstimate(
             flops=10 ** 9, bytes_accessed=8 * 10 ** 6, transcendentals=2 * 10 ** 5
         ),
-    )(tokens, phase_weight, phase_gain, unit_weight, unit_gain.reshape(1, width),
-      durations.reshape(1, rows))
+    )(*[pltpu.with_memory_space_constraint(a, pltpu.HBM) for a in (tokens, phase_weight, phase_gain, unit_weight, unit_gain.reshape(1, width),
+      durations.reshape(1, rows))])
 
 
 def solution(mesh):

time: 36 us -> 32.8 us (0.911)
  local copies, waits for them, and re-layouts: 3.44 us -> 1.45 us
  Pallas kernels: 31.7 us -> 30.5 us
    unnamed x2, local copies, waits for them, and re-layouts: 3.44 us -> 1.45 us
    pallas_call x1, Pallas kernels: 31.7 us -> 30.5 us  [shards(): pl.pallas_call(functools.partial(kernel, phases, seqsize, slow, mid, rows...]
where the time goes in v3:
time: 32.8 us; the launch traced here: 32.6 us
  Pallas kernels  30.5 us (93%)
  local copies, waits for them, and re-layouts  1.45 us (4%)
  between operations  0.64 us (2%)
    pallas_call x1, Pallas kernels, shards(): pl.pallas_call(functools.partial(kernel, phases, seqsize, slow, mid, rows...  30.5 us
    unnamed x2, local copies, waits for them, and re-layouts  1.45 us

profile of v3, /device:TPU:25, one launch (start us, length us, event | category | flops | bytes accessed | tf_op | source)
XLA Modules:
  0.0 32.6 jit_solution(13383811514066108012)
XLA Ops:
  0.6 30.5 %shard_map.77 = (bf16[64,1024]{1,0:T(8,128)(2,1)S(1)}, bf16[256,1024]{1,0:T(8,128)(2,1)S(1)}) custom-call(bf16[64,1024]{1,0:T(8,128)(2,1)} %tokens_hbm.1, bf16[1,1024,1024]{2,1,0:T(8,128)(2,1)} %weight.1, f32[1,1024]{1,0:T(1,128)} %gain_hbm.1, bf16[1024,1024]{1,0:T(8,128)(2,1)} %unit_weight.1, f32[1,1024]{1,0:T(1,128)} %bitcast.2, s32[1,64]{1,0:T(1,128)} %bitcast.3), custom_call_target="tpu_custom_call" | custom-call | flops 1000000000 | bytes 8000000 | tf_op jit(solution)/shard_map/pallas_call | solution.py:382
  31.2 0.7 %copy.10 = bf16[64,1024]{1,0:T(8,128)(2,1)} copy(bf16[64,1024]{1,0:T(8,128)(2,1)S(1)} %get-tuple-element.2) | data formatting | bytes 262144
  31.8 0.8 %copy.11 = bf16[256,1024]{1,0:T(8,128)(2,1)} copy(bf16[256,1024]{1,0:T(8,128)(2,1)S(1)} %get-tuple-element.3) | data formatting | bytes 1048576

commit v4 on v3

--- a/solution.py
+++ b/solution.py
@@ -47,14 +47,20 @@
     def seq_of(zz, yy, cc):
         return zz * plane + yy * 2 + cc
 
-    def bounds(zz):
-        f0 = (p * seqsize + zz * plane) * FR_DEV
-        f1 = f0 + plane * FR_DEV - 1
+    def needed(first, count):
+        f0 = (p * seqsize + first) * FR_DEV
+        f1 = f0 + count * FR_DEV - 1
         low = jnp.maximum(f0 // dmax, toks - (frames - f0) // dmin)
         high = jnp.minimum(f1 // dmin, toks - ((frames - f1 - 1) // dmax + 1))
-        low = jnp.minimum(low // rows, zz * plane)
-        high = jnp.maximum(high // rows, zz * plane + plane - 1)
-        return low, high
+        return low // rows, high // rows
+
+    def bounds(zz):
+        low, high = needed(zz * plane, plane)
+        return jnp.minimum(low, zz * plane), jnp.maximum(high, zz * plane + plane - 1)
+
+    def chip_wants(b, o=0):
+        chip_low, chip_high = needed(seq_of(z, (y + o) % mid, 0), 2)
+        return (b >= chip_low) & (b <= chip_high)
 
     low, high = bounds(z)
     low_up, _ = bounds(z + 1)
@@ -88,7 +94,7 @@
     dur_all[s] = own[0:1, :]
 
     for b in range(seqsize):
-        @pl.when((b < low) | (b > high))
+        @pl.when(jnp.logical_not(chip_wants(b)))
         def _():
             held[b * rows:(b + 1) * rows, :] = jnp.zeros((rows, width), BF)
 
@@ -249,9 +255,15 @@
         def _():
             down(zz, h).start()
 
+        b = seq_of(zz, y, c)
         for o in range(1, mid):
-            across(zz, o, h).start()
-        sibling(seq_of(zz, y, c), h).start()
+            @pl.when(chip_wants(b, o))
+            def _():
+                across(zz, o, h).start()
+
+        @pl.when(chip_wants(b))
+        def _():
+            sibling(b, h).start()
 
     load_wu.wait()
 
@@ -274,7 +286,7 @@
         for o in range(1, mid):
             b = seq_of(zz, (y + o) % mid, c)
 
-            @pl.when(valid(zz) & wanted(b))
+            @pl.when(valid(zz) & chip_wants(b))
             def _():
                 arrived(b, h)
                 sibling(b, h).start()
@@ -284,7 +296,7 @@
             for yy in range(mid):
                 b = seq_of(zz, yy, 1 - c)
 
-                @pl.when(wanted(b))
+                @pl.when(chip_wants(b))
                 def _():
                     arrived(b, h)
 
@@ -301,7 +313,9 @@
         if first:
             work()
         else:
-            pl.when(valid(zz) & (zz * plane + plane - 1 >= low) & (zz * plane <= high))(work)
+            chip_low, chip_high = needed(seq_of(z, y, 0), 2)
+            pl.when(valid(zz) & (zz * plane + plane - 1 >= chip_low)
+                    & (zz * plane <= chip_high))(work)
 
     pl.when(last)(make_member)
     out_copies = []
@@ -355,12 +369,14 @@
                     down(zz, h).wait_send()
 
                 for o in range(1, mid):
-                    across(zz, o, h).wait_send()
+                    @pl.when(chip_wants(seq_of(zz, y, c), o))
+                    def _():
+                        across(zz, o, h).wait_send()
 
         for yy in range(mid):
             b = seq_of(zz, yy, c)
 
-            @pl.when(wanted(b))
+            @pl.when(chip_wants(b))
             def _():
                 for h in range(HALVES):
                     sibling(b, h).wait_send()

time: 32.8 us -> 32.9 us (level)
  no operation moved by 1% of the time
where the time goes in v4:
time: 32.9 us; the launch traced here: 32.7 us
  Pallas kernels  30.7 us (93%)
  local copies, waits for them, and re-layouts  1.45 us (4%)
  between operations  0.64 us (2%)
    pallas_call x1, Pallas kernels, shards(): pl.pallas_call(functools.partial(kernel, phases, seqsize, slow, mid, rows...  30.7 us
    unnamed x2, local copies, waits for them, and re-layouts  1.45 us

profile of v4, /device:TPU:25, one launch (start us, length us, event | category | flops | bytes accessed | tf_op | source)
XLA Modules:
  0.0 32.7 jit_solution(9342299221328065794)
XLA Ops:
  0.6 30.7 %shard_map.77 = (bf16[64,1024]{1,0:T(8,128)(2,1)S(1)}, bf16[256,1024]{1,0:T(8,128)(2,1)S(1)}) custom-call(bf16[64,1024]{1,0:T(8,128)(2,1)} %tokens_hbm.1, bf16[1,1024,1024]{2,1,0:T(8,128)(2,1)} %weight.1, f32[1,1024]{1,0:T(1,128)} %gain_hbm.1, bf16[1024,1024]{1,0:T(8,128)(2,1)} %unit_weight.1, f32[1,1024]{1,0:T(1,128)} %bitcast.2, s32[1,64]{1,0:T(1,128)} %bitcast.3), custom_call_target="tpu_custom_call" | custom-call | flops 1000000000 | bytes 8000000 | tf_op jit(solution)/shard_map/pallas_call | solution.py:398
  31.3 0.7 %copy.10 = bf16[64,1024]{1,0:T(8,128)(2,1)} copy(bf16[64,1024]{1,0:T(8,128)(2,1)S(1)} %get-tuple-element.2) | data formatting | bytes 262144
  32.0 0.8 %copy.11 = bf16[256,1024]{1,0:T(8,128)(2,1)} copy(bf16[256,1024]{1,0:T(8,128)(2,1)S(1)} %get-tuple-element.3) | data formatting | bytes 1048576

commit v5 on v4

--- a/solution.py
+++ b/solution.py
@@ -320,20 +320,17 @@
     pl.when(last)(make_member)
     out_copies = []
     steps = [(k, h) for k in range(slow) for h in range(HALVES)]
-    for i in range(HALVES, len(steps) + 4):
+    for i in range(HALVES, len(steps) + 5):
         if i < len(steps):
             k, h = steps[i]
             column(z - k, h)
             column(z + k, h)
-        if i == HALVES:
-            for h in range(HALVES - 1):
-                from_across(z, h)
-        if i - 1 < len(steps):
-            k, h = steps[i - 1]
+        if 0 <= i - 2 < len(steps):
+            k, h = steps[i - 2]
             for zz in (z - k, z + k) if k else (z,):
                 from_across(zz, h)
-        if 0 <= i - 4 < len(steps):
-            k, h = steps[i - 4]
+        if 0 <= i - 5 < len(steps):
+            k, h = steps[i - 5]
             for zz in (z - k, z + k) if k else (z,):
                 add_plane(zz, h, k == 0)
             if k == slow - 1:

time: 32.9 us -> 31 us (0.942)
  Pallas kernels: 30.7 us -> 28.7 us
    pallas_call x1, Pallas kernels: 30.7 us -> 28.7 us  [shards(): pl.pallas_call(functools.partial(kernel, phases, seqsize, slow, mid, rows...]
where the time goes in v5:
time: 31 us; the launch traced here: 30.8 us
  Pallas kernels  28.7 us (93%)
  local copies, waits for them, and re-layouts  1.45 us (5%)
  between operations  0.64 us (2%)
    pallas_call x1, Pallas kernels, shards(): pl.pallas_call(functools.partial(kernel, phases, seqsize, slow, mid, rows...  28.7 us
    unnamed x2, local copies, waits for them, and re-layouts  1.45 us

profile of v5, /device:TPU:25, one launch (start us, length us, event | category | flops | bytes accessed | tf_op | source)
XLA Modules:
  0.0 30.8 jit_solution(5098337483779186743)
XLA Ops:
  0.6 28.7 %shard_map.77 = (bf16[64,1024]{1,0:T(8,128)(2,1)S(1)}, bf16[256,1024]{1,0:T(8,128)(2,1)S(1)}) custom-call(bf16[64,1024]{1,0:T(8,128)(2,1)} %tokens_hbm.1, bf16[1,1024,1024]{2,1,0:T(8,128)(2,1)} %weight.1, f32[1,1024]{1,0:T(1,128)} %gain_hbm.1, bf16[1024,1024]{1,0:T(8,128)(2,1)} %unit_weight.1, f32[1,1024]{1,0:T(1,128)} %bitcast.2, s32[1,64]{1,0:T(1,128)} %bitcast.3), custom_call_target="tpu_custom_call" | custom-call | flops 1000000000 | bytes 8000000 | tf_op jit(solution)/shard_map/pallas_call | solution.py:395
  29.4 0.7 %copy.10 = bf16[64,1024]{1,0:T(8,128)(2,1)} copy(bf16[64,1024]{1,0:T(8,128)(2,1)S(1)} %get-tuple-element.2) | data formatting | bytes 262144
  30.0 0.8 %copy.11 = bf16[256,1024]{1,0:T(8,128)(2,1)} copy(bf16[256,1024]{1,0:T(8,128)(2,1)S(1)} %get-tuple-element.3) | data formatting | bytes 1048576
